TPU v7x, 256 devices: a whole 4x4x8 slice. The times are simulated.
256 devices in a mesh: grp: 8 (over z_lo, core), exp: 32 (over z_hi, y, x).
Axes of the slice: x: 4, y: 4, z: 8 (z_hi: 2, z_lo: 4; z = z_hi * 4 + z_lo), core: 2. Of those that a mesh axis runs over, the one named last changes fastest.
Arguments:
- tokens: bfloat16 [8192, 7168], P('exp', 'grp'), may hold values from -6 to 6
- d_out: bfloat16 [8192, 7168], P('exp', 'grp'), may hold values from -6 to 6
- row_expert: int32 [8192], P('exp'), may hold values from 0 to 31, as said below
- w_gate_up: bfloat16 [32, 7168, 2, 1024], P('exp', 'grp'), may hold values from -0.0625 to 0.0625
- w_down: bfloat16 [32, 1024, 7168], P('exp', None, 'grp'), may hold values from -0.1875 to 0.1875
Outputs:
- token_grads: bfloat16 [8192, 7168], P('exp', 'grp')
- gate_up_grads: bfloat16 [32, 7168, 2, 1024], P('exp', 'grp')
- down_grads: bfloat16 [32, 1024, 7168], P('exp', None, 'grp')
Inputs may be any that keep to these rules, and one draw needn't show every extreme that they name: `row_expert`: in each block of 256 rows held by one index of exp, one expert, the same for every block, is named by exactly 32 rows; every other expert by at most 16 rows, and in every block some expert by exactly 16.
All inputs are finite; a program needn't handle non-finite values.
Results may differ from a plain program's by a relative error of at most 0.028.
Values may be sent and summed in bfloat16 or wider, within the bound.
A program may use at most 128 MiB of HBM per device.

v0:
```python
import jax
import jax.numpy as jnp
from jax import lax
from jax.sharding import PartitionSpec as P


def slot_ranks(row_expert, expert_count):
    onehot = (row_expert[:, None] == jnp.arange(expert_count, dtype=jnp.int32)[None, :]).astype(
        jnp.int32
    )
    running = jnp.cumsum(onehot, axis=0) - 1
    return (jnp.sum(running * onehot, axis=1), jnp.sum(onehot, axis=0))


def place_rows(source_rows, slot_index, slot_total):
    blank_rows = jnp.zeros((slot_total, source_rows.shape[1]), source_rows.dtype)
    return blank_rows.at[slot_index].set(source_rows, mode="drop")


def partial_products(rows_in, grads_in, local_gate_up, local_down):
    gate_up = jnp.dot(rows_in, local_gate_up, preferred_element_type=jnp.float32)
    hidden_grads = lax.dot_general(
        grads_in, local_down, (((1,), (1,)), ((), ())), preferred_element_type=jnp.float32
    )
    return (gate_up, hidden_grads)


def activate(gate_up, hidden_grads):
    hidden_width = hidden_grads.shape[1]
    gate_value = gate_up[:, :hidden_width]
    upward = gate_up[:, hidden_width:]
    sigmoid_value = jax.nn.sigmoid(gate_value)
    activated = gate_value * sigmoid_value
    gate_slope = sigmoid_value * (1.0 + gate_value * (1.0 - sigmoid_value))
    hidden = (activated * upward).astype(jnp.bfloat16)
    branch = jnp.concatenate(
        [hidden_grads * upward * gate_slope, hidden_grads * activated], axis=1
    ).astype(jnp.bfloat16)
    return (hidden, branch)


def outer_terms(rows_in, grads_in, hidden, branch, local_gate_up):
    down_part = lax.dot_general(
        hidden, grads_in, (((0,), (0,)), ((), ())), preferred_element_type=jnp.float32
    )
    gate_up_part = lax.dot_general(
        rows_in, branch, (((0,), (0,)), ((), ())), preferred_element_type=jnp.float32
    )
    row_grads = lax.dot_general(
        branch, local_gate_up, (((1,), (1,)), ((), ())), preferred_element_type=jnp.float32
    ).astype(jnp.bfloat16)
    return (gate_up_part, down_part, row_grads)


def finish_rows(rows_in, grads_in, gate_up, hidden_grads, local_gate_up):
    hidden, branch = activate(gate_up, hidden_grads)
    return outer_terms(rows_in, grads_in, hidden, branch, local_gate_up)


def local(tokens, d_out, row_expert, w_gate_up, w_down):
    row_count, feature_share = tokens.shape
    hidden_width = w_down.shape[1]
    expert_count = lax.axis_size("exp")
    local_gate_up = w_gate_up.reshape(feature_share, 2 * hidden_width)
    local_down = w_down.reshape(hidden_width, feature_share)
    slot_rank, expert_loads = slot_ranks(row_expert, expert_count)
    hot_cap = 4 * row_count // expert_count
    slot_index = row_expert * hot_cap + slot_rank
    slot_total = expert_count * hot_cap
    sent_rows, sent_grads = (
        lax.all_to_all(
            place_rows(tokens, slot_index, slot_total).reshape(
                expert_count, hot_cap, feature_share
            ),
            "exp",
            split_axis=0,
            concat_axis=0,
            tiled=True,
        ),
        lax.all_to_all(
            place_rows(d_out, slot_index, slot_total).reshape(expert_count, hot_cap, feature_share),
            "exp",
            split_axis=0,
            concat_axis=0,
            tiled=True,
        ),
    )
    rows_in = sent_rows.reshape(slot_total, feature_share)
    grads_in = sent_grads.reshape(slot_total, feature_share)
    gate_part, hidden_part = partial_products(rows_in, grads_in, local_gate_up, local_down)
    gate_up, hidden_grads = (
        lax.psum(gate_part.astype(jnp.bfloat16), "grp").astype(jnp.float32),
        lax.psum(hidden_part.astype(jnp.bfloat16), "grp").astype(jnp.float32),
    )
    gate_up_part, down_part, row_grads = finish_rows(
        rows_in, grads_in, gate_up, hidden_grads, local_gate_up
    )
    returned = lax.all_to_all(
        row_grads.reshape(expert_count, hot_cap, feature_share),
        "exp",
        split_axis=0,
        concat_axis=0,
        tiled=True,
    )
    token_grads = returned.reshape(slot_total, feature_share)[slot_index]
    gate_up_grads = gate_up_part.astype(jnp.bfloat16).reshape(1, feature_share, 2, hidden_width)
    down_grads = down_part.astype(jnp.bfloat16).reshape(1, hidden_width, feature_share)
    return (token_grads, gate_up_grads, down_grads)


def solution(mesh):
    return jax.shard_map(
        local,
        mesh=mesh,
        in_specs=(
            P("exp", "grp"),
            P("exp", "grp"),
            P("exp"),
            P("exp", "grp", None, None),
            P("exp", None, "grp"),
        ),
        out_specs=(P("exp", "grp"), P("exp", "grp", None, None), P("exp", None, "grp")),
        check_vma=False,
    )
```

profile of v0, /device:TPU:24, one launch (start us, length us, event | category | flops | bytes accessed | tf_op | source)
XLA Modules:
  0.0 349.3 jit_solution(7992478722531022992)
XLA Ops:
  7.2 0.0 copy-start
  7.2 0.8 fusion.15
  8.0 0.6 reduce-window.6
  8.6 0.2 slice_reduce_fusion
  8.8 0.8 fusion.14
  9.6 0.7 compare_select_fusion
  10.3 3.5 %scatter_custom_fusion = bf16[1024,896]{1,0:T(8,128)(2,1)} fusion(s32[256]{0:T(256)S(1)} %compare_select_fusion, bf16[256,896]{1,0:T(8,128)(2,1)} %param.6, bf16[]{:T(256)} %constant.6.clone.1), kind=kCustom, calls=%fused_computation.22 | custom fusion | bytes 1835520 | tf_op jit(solution)/shard_map/scatter | solution.py:17
  13.8 14.0 %all-to-all-start = ((bf16[32,32,896]{2,1,0:T(8,128)(2,1)}), bf16[32,32,896]{2,1,0:T(8,128)(2,1)}, u32[]{:S(2)}, u32[]{:S(2)}) async-start(bf16[32,32,896]{2,1,0:T(8,128)(2,1)} %bitcast.37), calls=%async_computation | async-start | bytes 3670016 | tf_op jit(solution)/shard_map/all_to_all | solution.py:80
  27.8 3.6 %scatter_custom_fusion.1 = bf16[1024,896]{1,0:T(8,128)(2,1)} fusion(s32[256]{0:T(256)S(1)} %compare_select_fusion, bf16[256,896]{1,0:T(8,128)(2,1)} %param.5, bf16[]{:T(256)} %constant.6.clone.1), kind=kCustom, calls=%fused_computation.20 | custom fusion | bytes 1835520 | tf_op jit(solution)/shard_map/scatter | solution.py:17
  31.4 40.7 %all-to-all-done = bf16[32,32,896]{2,1,0:T(8,128)(2,1)} async-done(((bf16[32,32,896]{2,1,0:T(8,128)(2,1)}), bf16[32,32,896]{2,1,0:T(8,128)(2,1)}, u32[]{:S(2)}, u32[]{:S(2)}) %all-to-all-start) | async-done | bytes 1835040 | tf_op jit(solution)/shard_map/all_to_all | solution.py:80
  72.1 7.4 %all-to-all-start.1 = ((bf16[32,32,896]{2,1,0:T(8,128)(2,1)}), bf16[32,32,896]{2,1,0:T(8,128)(2,1)}, u32[]{:S(2)}, u32[]{:S(2)}) async-start(bf16[32,32,896]{2,1,0:T(8,128)(2,1)} %bitcast.36), calls=%async_computation.1 | async-start | bytes 3670016 | tf_op jit(solution)/shard_map/all_to_all | solution.py:71
  79.6 0.2 all-reduce.3.cloned.1.call-start
  79.8 5.1 %copy.10 = bf16[112,8,2,1024]{3,1,2,0:T(8,128)(2,1)} copy(bf16[112,8,2,1024]{3,2,1,0:T(2,128)(2,1)} %bitcast.38) | data formatting | bytes 7340032
  84.9 0.0 copy-done
  84.9 5.2 %convolution_convert_fusion.2 = bf16[1024,1024]{1,0:T(8,128)(2,1)} fusion(bf16[1024,896]{1,0:T(8,128)(2,1)} %bitcast.3, bf16[1,1024,896]{2,1,0:T(8,128)(2,1)S(1)} %copy-done), kind=kOutput, calls=%fused_computation.16 | convolution fusion | flops 1880096768 | bytes 5767168 | tf_op jit(solution)/shard_map/dot_general | solution.py:22
  90.1 17.8 %all-to-all-done.1 = bf16[32,32,896]{2,1,0:T(8,128)(2,1)} async-done(((bf16[32,32,896]{2,1,0:T(8,128)(2,1)}), bf16[32,32,896]{2,1,0:T(8,128)(2,1)}, u32[]{:S(2)}, u32[]{:S(2)}) %all-to-all-start.1) | async-done | bytes 1835040 | tf_op jit(solution)/shard_map/all_to_all | solution.py:71
  107.9 9.1 %convolution_convert_fusion = bf16[1024,2048]{1,0:T(8,128)(2,1)} fusion(bf16[1024,896]{1,0:T(8,128)(2,1)} %bitcast.6, bf16[896,2048]{1,0:T(8,128)(2,1)} %bitcast.39), kind=kOutput, calls=%fused_computation.12 | convolution fusion | flops 3760193536 | bytes 9699328 | tf_op jit(solution)/shard_map/dot_general | solution.py:21
  117.0 0.0 all-reduce.3.cloned.1.call-update
  117.0 155.6 %all-reduce.3.cloned.1.call-done = (bf16[1024,1024]{1,0:T(8,128)(2,1)}, bf16[1024,2048]{1,0:T(8,128)(2,1)}) async-done(((bf16[1024,1024]{1,0:T(8,128)(2,1)}, bf16[1024,2048]{1,0:T(8,128)(2,1)}), (bf16[1024,1024]{1,0:T(8,128)(2,1)}, bf16[1024,2048]{1,0:T(8,128)(2,1)})) %all-reduce.3.cloned.1.call-update) | async-done | bytes 6291472 | tf_op jit(solution)/shard_map/psum | solution.py:93
  272.6 0.0 copy-start.3
  272.6 3.4 convert_element_type.34
  276.0 0.0 copy-start.1
  276.0 0.0 copy-done.3
  276.0 0.0 copy-start.2
  276.1 2.6 fusion.1
  278.7 1.5 copy-done.1
  280.2 0.0 copy-start.4
  280.2 0.0 copy-start.5
  280.2 0.7 copy-done.2
  280.9 5.7 %fusion.7 = bf16[1024,896]{1,0:T(8,128)(2,1)} fusion(bf16[896,2048]{1,0:T(8,128)(2,1)S(1)} %bitcast.40, bf16[1024,1024]{1,0:T(8,128)(2,1)S(1)} %get-tuple-element.6, bf16[1024,1024]{1,0:T(8,128)(2,1)S(1)} %get-tuple-element.5), kind=kOutput, calls=%fused_computation.19 | convolution fusion | flops 3767402496 | bytes 9699328 | tf_op jit(solution)/shard_map/dot_general | solution.py:49
  286.6 0.0 copy-done.4
  286.6 0.0 copy-done.5
  286.6 9.9 %all-to-all-start.2 = ((bf16[32,32,896]{2,1,0:T(8,128)(2,1)}), bf16[32,32,896]{2,1,0:T(8,128)(2,1)}, u32[]{:S(2)}, u32[]{:S(2)}) async-start(bf16[32,32,896]{2,1,0:T(8,128)(2,1)} %bitcast.41), calls=%async_computation.2 | async-start | bytes 3670016 | tf_op jit(solution)/shard_map/all_to_all | solution.py:98
  296.5 8.7 %convolution_convert_fusion.1 = bf16[896,2048]{1,0:T(8,128)(2,1)} fusion(bf16[1024,896]{1,0:T(8,128)(2,1)} %bitcast.6, bf16[1024,1024]{1,0:T(8,128)(2,1)} %copy-done.5, bf16[1024,1024]{1,0:T(8,128)(2,1)} %copy-done.4), kind=kOutput, calls=%fused_computation.13 | convolution fusion | flops 3768320000 | bytes 9699328 | tf_op jit(solution)/shard_map/dot_general | solution.py:46
  305.1 7.1 %reshape.63 = bf16[1,896,2,1024]{3,2,1,0:T(2,128)(2,1)} reshape(bf16[896,2048]{1,0:T(8,128)(2,1)} %convolution_convert_fusion.1) | data formatting | bytes 7340032 | tf_op jit(solution)/shard_map/reshape | solution.py:106
  312.3 7.7 %convert_bitcast_fusion = bf16[1,1024,896]{2,1,0:T(8,128)(2,1)} fusion(bf16[1024,896]{1,0:T(8,128)(2,1)} %bitcast.3, f32[1024,2048]{1,0:T(8,128)} %copy-done.1), kind=kOutput, calls=%fused_computation.18 | convolution fusion | flops 1886257152 | bytes 12058624 | tf_op jit(solution)/shard_map/dot_general | solution.py:43
  319.9 18.6 %all-to-all-done.2 = bf16[32,32,896]{2,1,0:T(8,128)(2,1)} async-done(((bf16[32,32,896]{2,1,0:T(8,128)(2,1)}), bf16[32,32,896]{2,1,0:T(8,128)(2,1)}, u32[]{:S(2)}, u32[]{:S(2)}) %all-to-all-start.2) | async-done | bytes 1835040 | tf_op jit(solution)/shard_map/all_to_all | solution.py:98
  338.5 4.0 %gather_fusion = bf16[256,896]{1,0:T(8,128)(2,1)} fusion(bf16[1024,896]{1,0:T(8,128)(2,1)} %bitcast.8, s32[1024]{0:T(1024)S(1)} %pad_clamp_fusion), kind=kCustom, calls=%fused_computation | custom fusion | bytes 918528 | tf_op jit(solution)/shard_map/gather | solution.py:105
  (3 shorter events, 0.0 us)
Async XLA Ops:
  7.2 77.7 %copy-start = (bf16[1,1024,896]{2,1,0:T(8,128)(2,1)S(1)}, bf16[1,1024,896]{2,1,0:T(8,128)(2,1)}, u32[]{:S(2)}) copy-start(bf16[1,1024,896]{2,1,0:T(8,128)(2,1)} %param.9) | copy-start | bytes 5505028
  13.8 58.3 %all-to-all-start = ((bf16[32,32,896]{2,1,0:T(8,128)(2,1)}), bf16[32,32,896]{2,1,0:T(8,128)(2,1)}, u32[]{:S(2)}, u32[]{:S(2)}) async-start(bf16[32,32,896]{2,1,0:T(8,128)(2,1)} %bitcast.37), calls=%async_computation | async-start | bytes 3670016 | tf_op jit(solution)/shard_map/all_to_all | solution.py:80
  72.1 35.8 %all-to-all-start.1 = ((bf16[32,32,896]{2,1,0:T(8,128)(2,1)}), bf16[32,32,896]{2,1,0:T(8,128)(2,1)}, u32[]{:S(2)}, u32[]{:S(2)}) async-start(bf16[32,32,896]{2,1,0:T(8,128)(2,1)} %bitcast.36), calls=%async_computation.1 | async-start | bytes 3670016 | tf_op jit(solution)/shard_map/all_to_all | solution.py:71
  79.6 193.0 %all-reduce.3.cloned.1.call-start = ((), (), s32[]{:S(2)}) async-start(), calls=%async_computation.3 | async-start | bytes 12582912 | tf_op jit(solution)/shard_map/psum | solution.py:93
  272.6 3.4 copy-start.3
  276.0 4.1 %copy-start.1 = (f32[1024,2048]{1,0:T(8,128)}, f32[1024,2048]{1,0:T(8,128)S(1)}, u32[]{:S(2)}) copy-start(f32[1024,2048]{1,0:T(8,128)S(1)} %convert_element_type.34) | copy-start | bytes 25165828
  276.0 4.8 %copy-start.2 = (bf16[112,8,2,1024]{3,1,2,0:T(8,128)(2,1)S(1)}, bf16[112,8,2,1024]{3,1,2,0:T(8,128)(2,1)}, u32[]{:S(2)}) copy-start(bf16[112,8,2,1024]{3,1,2,0:T(8,128)(2,1)} %copy.10) | copy-start | bytes 11010052
  280.2 6.4 %copy-start.4 = (bf16[1024,1024]{1,0:T(8,128)(2,1)}, bf16[1024,1024]{1,0:T(8,128)(2,1)S(1)}, u32[]{:S(2)}) copy-start(bf16[1024,1024]{1,0:T(8,128)(2,1)S(1)} %get-tuple-element.5) | copy-start | bytes 6291460
  280.2 6.4 %copy-start.5 = (bf16[1024,1024]{1,0:T(8,128)(2,1)}, bf16[1024,1024]{1,0:T(8,128)(2,1)S(1)}, u32[]{:S(2)}) copy-start(bf16[1024,1024]{1,0:T(8,128)(2,1)S(1)} %get-tuple-element.6) | copy-start | bytes 6291460
  286.6 52.0 %all-to-all-start.2 = ((bf16[32,32,896]{2,1,0:T(8,128)(2,1)}), bf16[32,32,896]{2,1,0:T(8,128)(2,1)}, u32[]{:S(2)}, u32[]{:S(2)}) async-start(bf16[32,32,896]{2,1,0:T(8,128)(2,1)} %bitcast.41), calls=%async_computation.2 | async-start | bytes 3670016 | tf_op jit(solution)/shard_map/all_to_all | solution.py:98
Sparse Core Ops, SparseCore 0:
  117.1 155.4 all-reduce.2
where the time goes:
time: 356 us; the launch traced here: 349 us
  waiting for transfers between devices  233 us (65%)
  matrix products  36.2 us (10%)
  starting transfers between devices  31.5 us (9%)
  local copies, waits for them, and re-layouts  25.8 us (7%)
  between operations  14.1 us (4%)
  other arithmetic  8.9 us (2%)
    psum x1, waiting for transfers between devices, local(): lax.psum(hidden_part.astype(jnp.bfloat16), 'grp').astype(jnp.float32)  156 us
    all_to_all x1, waiting for transfers between devices, local(): lax.all_to_all(place_rows(d_out, slot_index, slot_total).reshape(expert_c...  40.7 us
    all_to_all x1, waiting for transfers between devices, local(): lax.all_to_all(row_grads.reshape(expert_count, hot_cap, feature_share), '...  18.6 us
    all_to_all x1, waiting for transfers between devices, local(): lax.all_to_all(place_rows(tokens, slot_index, slot_total).reshape(expert_...  17.8 us
    all_to_all x1, starting transfers between devices, local(): lax.all_to_all(place_rows(d_out, slot_index, slot_total).reshape(expert_c...  14 us
    all_to_all x1, starting transfers between devices, local(): lax.all_to_all(row_grads.reshape(expert_count, hot_cap, feature_share), '...  9.89 us
    dot_general x1, matrix products, partial_products(): jnp.dot(rows_in, local_gate_up, preferred_element_type=jnp.float32)  9.06 us
    dot_general x1, matrix products, outer_terms(): lax.dot_general(rows_in, branch, (((0,), (0,)), ((), ())), preferred_elem...  8.66 us
  transfers between devices with their start and end apart: 4, of which 4 were waited for; matrix products, arithmetic and copies ran while one was open for 11% of the time, Pallas kernels for 0%

commit v1 on v0

v1 whole, which is shorter than its diff:
```python
import jax
import jax.numpy as jnp
from jax import lax
from jax.experimental import pallas as pl
from jax.experimental.pallas import tpu as pltpu
from jax.sharding import PartitionSpec as P

MESH = pl.DeviceIdType.MESH
F32 = jnp.float32
BF16 = jnp.bfloat16

ROWS = 256
FEAT = 896
HID = 1024
WIDE = 3 * HID
N_EXP = 32
HALF = 16
CAP = 16
BASE = N_EXP * CAP
SLOTS = 2 * BASE
CHUNKS = 4
CHUNK = SLOTS // CHUNKS
SHARE = CHUNK // 2
UNIT = SHARE // 4
TILE = 512

NN = (((1,), (0,)), ((), ()))
NT = (((1,), (1,)), ((), ()))
TN = (((0,), (0,)), ((), ()))


def mm(a, b, dims=NN):
    return lax.dot_general(a, b, dims, preferred_element_type=F32)


def rows(start, size):
    return pl.ds(pl.multiple_of(start, 16), size)


def kernel(
    expert_ref, tok_ref, dout_ref, wgu_hbm, wd_hbm,
    tg_ref, gug_ref, dg_ref,
    wgu, wd, xin, din, sendx, sendd, ovx, ovd, csend, crecv, acc,
    rs_send, rs_recv, hb, rowg, back, backo, zsend, zrecv, slots, hotm,
    w_sem, base_send, base_recv, ovz_send, ovz_recv, ov_send, ov_recv, c_send, c_recv,
    rs_s, rs_r, ag_s, ag_r, ret_s, ret_r, reto_s, reto_r, retz_s, retz_r,
):
    me_e = lax.axis_index("exp")
    me_g = lax.axis_index("grp")
    z = me_g // 2
    core = lax.rem(me_g, 2)
    half = me_e // HALF
    q = lax.rem(me_e, HALF)
    z_partner = {"exp": lax.rem(me_e + HALF, N_EXP)}
    core_partner = {"grp": me_g + 1 - 2 * core}
    right = {"grp": lax.rem(me_g + 2, 8)}
    left = {"grp": lax.rem(me_g + 6, 8)}

    def remote(src, dst, s_sem, r_sem, dev):
        return pltpu.make_async_remote_copy(
            src_ref=src, dst_ref=dst, send_sem=s_sem, recv_sem=r_sem, device_id=dev, device_id_type=MESH
        )

    def place(s):
        return (lax.rem(s, HALF) // 8) * 16 + (s // HALF) * 8 + lax.rem(s, 8)

    w1 = pltpu.make_async_copy(wgu_hbm, wgu, w_sem.at[0])
    w2 = pltpu.make_async_copy(wd_hbm, wd, w_sem.at[1])
    w1.start()
    w2.start()
    barrier = pltpu.get_barrier_semaphore()

    @pl.loop(1, N_EXP)
    def _(p):
        pl.semaphore_signal(
            barrier, inc=1, device_id={"exp": lax.rem(me_e + p, N_EXP)}, device_id_type=MESH
        )

    @pl.loop(1, 8)
    def _(p):
        pl.semaphore_signal(barrier, inc=1, device_id={"grp": lax.rem(me_g + p, 8)}, device_id_type=MESH)

    expert = expert_ref[...]
    e_iota = lax.broadcasted_iota(jnp.int32, (N_EXP, ROWS), 0)
    mine = (expert == e_iota).astype(F32)
    upto = (
        lax.broadcasted_iota(jnp.int32, (ROWS, ROWS), 0) <= lax.broadcasted_iota(jnp.int32, (ROWS, ROWS), 1)
    ).astype(F32).astype(BF16)
    running = mm(mine.astype(BF16), upto)
    rank = jnp.sum(running * mine, axis=0, keepdims=True) - 1.0
    slot = jnp.where(rank < CAP, expert.astype(F32) * CAP + rank, -1.0)
    over = rank - CAP
    slots[0:1, :] = slot
    slots[1:2, :] = over
    loads = jnp.sum(mine, axis=1, keepdims=True)
    is_me = (lax.broadcasted_iota(jnp.int32, (N_EXP, 1), 0) == me_e).astype(F32)
    hot = jnp.sum(jnp.where(loads > CAP + 0.5, 1.0, 0.0) * is_me, axis=0, keepdims=True)
    hotm[...] = jnp.broadcast_to(hot, (16, FEAT)).astype(BF16)

    def picks(start, size, values):
        at = lax.broadcasted_iota(jnp.int32, (size, ROWS), 0).astype(F32) + start
        return (at == values).astype(F32).astype(BF16)

    over_pick = picks(0.0, CAP, over)
    ovx[0:CAP, :] = mm(over_pick, tok_ref[...]).astype(BF16)
    ovd[0:CAP, :] = mm(over_pick, dout_ref[...]).astype(BF16)
    for b in range(BASE // 128):
        pick = picks(128.0 * b, 128, slot)
        sendx[b * 128 : (b + 1) * 128, :] = mm(pick, tok_ref[...]).astype(BF16)
        sendd[b * 128 : (b + 1) * 128, :] = mm(pick, dout_ref[...]).astype(BF16)
    pl.semaphore_wait(barrier, N_EXP - 1 + 7)

    ovz = [
        remote(buf.at[pl.ds(0, CAP)], buf.at[pl.ds(CAP, CAP)], ovz_send.at[n], ovz_recv.at[n], z_partner)
        for n, buf in enumerate((ovx, ovd))
    ]
    for copy in ovz:
        copy.start()
    my_place = place(me_e) * CAP

    @pl.loop(1, N_EXP)
    def _(p):
        to = lax.rem(me_e + p, N_EXP)
        for n, (src, dst) in enumerate(((sendx, xin), (sendd, din))):
            remote(
                src.at[rows(to * CAP, CAP)], dst.at[rows(my_place, CAP)],
                base_send.at[n], base_recv.at[n], {"exp": to},
            ).start()

    xin[rows(my_place, CAP), :] = sendx[rows(me_e * CAP, CAP), :]
    din[rows(my_place, CAP), :] = sendd[rows(me_e * CAP, CAP), :]
    for copy in ovz:
        copy.wait_recv()
    over_place = BASE + q * 2 * CAP

    @pl.loop(1, HALF)
    def _(p):
        to = half * HALF + lax.rem(q + p, HALF)
        for n, (src, dst) in enumerate(((ovx, xin), (ovd, din))):
            remote(
                src, dst.at[rows(over_place, 2 * CAP)], ov_send.at[n], ov_recv.at[n], {"exp": to}
            ).start()

    xin[rows(over_place, 2 * CAP), :] = ovx[...]
    din[rows(over_place, 2 * CAP), :] = ovd[...]

    def many(buf, count, s_sem, r_sem):
        part = buf.at[pl.ds(0, count)]
        return remote(part, part, s_sem, r_sem, z_partner)

    w1.wait()
    w2.wait()
    many(xin, BASE - CAP, base_send.at[0], base_recv.at[0]).wait_recv()
    many(din, BASE - CAP, base_send.at[1], base_recv.at[1]).wait_recv()

    ends = []

    def partials(k, mine_too):
        start = k * CHUNK + SHARE * (core if mine_too else 1 - core)

        def put(value, col):
            if mine_too:
                acc[pl.ds(k * SHARE, SHARE), col] = value
            else:
                csend[pl.ds(k * SHARE, SHARE), col] = value.astype(BF16)

        @pl.loop(0, 2 * HID // TILE)
        def _(n):
            col = pl.ds(pl.multiple_of(n * TILE, TILE), TILE)
            put(mm(xin[rows(start, SHARE), :], wgu[:, col]), col)

        @pl.loop(0, HID // TILE)
        def _(n):
            out = pl.ds(pl.multiple_of(2 * HID + n * TILE, TILE), TILE)
            put(mm(din[rows(start, SHARE), :], wd[rows(n * TILE, TILE), :], NT), out)

    def core_copy(k):
        part = pl.ds(k * SHARE, SHARE)
        return remote(csend.at[part], crecv.at[part], c_send.at[k], c_recv.at[k], core_partner)

    def stage_p(k):
        partials(k, False)
        core_copy(k).start()
        partials(k, True)

    def stage_c(k):
        core_copy(k).wait_recv()

        @pl.loop(0, SHARE // 16)
        def _(n):
            at = rows(k * SHARE + n * 16, 16)
            acc[at, :] += crecv[at, :].astype(F32)

    def rs_copy(k, way, d):
        part = pl.ds(((k * 2 + way) * 4 + d) * UNIT, UNIT)
        return remote(
            rs_send.at[part], rs_recv.at[part], rs_s.at[k, way, d], rs_r.at[k, way, d], (right, left)[way]
        )


    def rs_forward(k, way, d, first):
        at = k * SHARE + d * UNIT
        part = ((k * 2 + way) * 4 + d) * UNIT
        copy = rs_copy(k, way, d)
        if not first:
            copy.wait_recv()

        @pl.loop(0, UNIT // 16)
        def _(n):
            value = acc[rows(at + n * 16, 16), :]
            if not first:
                value = value + rs_recv[rows(part + n * 16, 16), :].astype(F32)
            rs_send[rows(part + n * 16, 16), :] = value.astype(BF16)

        copy.start()

    def stage_e(k):
        @pl.when(z == 0)
        def _():
            for d in (3, 2, 1):
                rs_forward(k, 0, d, True)

        @pl.when(z == 3)
        def _():
            for d in (0, 1, 2):
                rs_forward(k, 1, d, True)

    def stage_m(k):
        @pl.when(z == 1)
        def _():
            rs_forward(k, 0, 3, False)
            rs_forward(k, 0, 2, False)
            rs_forward(k, 1, 0, False)

        @pl.when(z == 2)
        def _():
            rs_forward(k, 1, 0, False)
            rs_forward(k, 1, 1, False)
            rs_forward(k, 0, 3, False)

    def ag_copy(k, way, j):
        part = rows(k * CHUNK + core * SHARE + j * UNIT, UNIT)
        return remote(
            hb.at[part], hb.at[part], ag_s.at[k, way, j], ag_r.at[k, core, j], (right, left, core_partner)[way]
        )

    def stage_f(k):
        at = k * SHARE + z * UNIT

        def fold(way):
            dyn = rows(((k * 2 + way) * 4 + z) * UNIT, UNIT)
            remote(
                rs_send.at[dyn], rs_recv.at[dyn], rs_s.at[k, way, z], rs_r.at[k, way, z], (right, left)[way]
            ).wait_recv()
            acc[rows(at, UNIT), :] += rs_recv[dyn, :].astype(F32)

        @pl.when(z > 0)
        def _():
            fold(0)

        @pl.when(z < 3)
        def _():
            fold(1)

        out = rows(k * CHUNK + core * SHARE + z * UNIT, UNIT)

        @pl.loop(0, HID // 256)
        def _(n):
            c0 = pl.multiple_of(n * 256, 256)
            gate = acc[rows(at, UNIT), pl.ds(c0, 256)]
            up = acc[rows(at, UNIT), pl.ds(c0 + HID, 256)]
            grad = acc[rows(at, UNIT), pl.ds(c0 + 2 * HID, 256)]
            sig = jax.nn.sigmoid(gate)
            act = gate * sig
            slope = sig * (1.0 + gate * (1.0 - sig))
            hb[out, pl.ds(c0, 256)] = (act * up).astype(BF16)
            hb[out, pl.ds(c0 + HID, 256)] = (grad * up * slope).astype(BF16)
            hb[out, pl.ds(c0 + 2 * HID, 256)] = (grad * act).astype(BF16)

        @pl.when(z < 3)
        def _():
            ag_copy(k, 0, z).start()

        @pl.when(z > 0)
        def _():
            ag_copy(k, 1, z).start()

        ag_copy(k, 2, z).start()

    def stage_a(k):
        for dist in (1, 2, 3):
            from_left = z - dist
            from_right = z + dist

            @pl.when(from_left >= 0)
            def _():
                ag_copy(k, 0, from_left).wait_recv()

                @pl.when(z < 3)
                def _():
                    ag_copy(k, 0, from_left).start()

                ag_copy(k, 2, from_left).start()

            @pl.when(from_right <= 3)
            def _():
                ag_copy(k, 1, from_right).wait_recv()

                @pl.when(z > 0)
                def _():
                    ag_copy(k, 1, from_right).start()

                ag_copy(k, 2, from_right).start()

    def stage_g(k):
        for j in range(4):
            part = rows(k * CHUNK + (1 - core) * SHARE + j * UNIT, UNIT)
            remote(
                hb.at[part], hb.at[part], ag_s.at[k, 2, j], ag_r.at[k, 1 - core, j], core_partner
            ).wait_recv()
        here = pl.ds(k * CHUNK, CHUNK)
        for c0, size in ((0, 256), (256, 256), (512, 256), (768, 128)):
            rowg[here, c0 : c0 + size] = mm(hb[here, HID:], wgu[c0 : c0 + size, :], NT).astype(BF16)
        if k < 2:

            @pl.loop(0, 16)
            def _(p):
                at = lax.rem(q + p, 16)
                to = (at // 8) * HALF + k * 8 + lax.rem(at, 8)

                @pl.when(to != me_e)
                def _():
                    remote(
                        rowg.at[rows(k * CHUNK + at * CAP, CAP)], back.at[rows(me_e * CAP, CAP)],
                        ret_s, ret_r, {"exp": to},
                    ).start()

                @pl.when(to == me_e)
                def _():
                    back[rows(me_e * CAP, CAP), :] = rowg[rows(k * CHUNK + at * CAP, CAP), :]
        else:

            @pl.loop(0, 8)
            def _(p):
                at = lax.rem(q + p, 8)
                near = (k - 2) * 8 + at
                src = rows(k * CHUNK + at * 2 * CAP, 2 * CAP)

                @pl.when(near != q)
                def _():
                    remote(
                        rowg.at[src], backo.at[rows(q * 2 * CAP, 2 * CAP)],
                        reto_s, reto_r, {"exp": half * HALF + near},
                    ).start()

                @pl.when(near == q)
                def _():
                    backo[rows(q * 2 * CAP, 2 * CAP), :] = rowg[src, :]

    def hot_rows():
        many(xin, (HALF - 1) * 2 * CAP, ov_send.at[0], ov_recv.at[0]).wait_recv()
        many(din, (HALF - 1) * 2 * CAP, ov_send.at[1], ov_recv.at[1]).wait_recv()

        @pl.loop(0, BASE // 16)
        def _(n):
            at = rows(BASE + n * 16, 16)
            xin[at, :] = xin[at, :] * hotm[...]
            din[at, :] = din[at, :] * hotm[...]

    stage_p(0)
    stage_c(0)
    stage_e(0)
    stage_p(1)
    stage_c(1)
    stage_m(0)
    stage_e(1)
    stage_f(0)
    hot_rows()
    stage_p(2)
    stage_c(2)
    stage_m(1)
    stage_e(2)
    stage_a(0)
    stage_f(1)
    stage_p(3)
    stage_c(3)
    stage_g(0)
    stage_m(2)
    stage_e(3)
    stage_a(1)
    stage_f(2)
    stage_g(1)
    stage_m(3)
    stage_a(2)
    stage_f(3)
    stage_g(2)
    stage_a(3)
    stage_g(3)

    def gate_up_grads():
        @pl.loop(0, 2 * HID // TILE)
        def _(n):
            c0 = pl.multiple_of(n * TILE, TILE)
            for f0, size in ((0, 256), (256, 256), (512, 256), (768, 128)):
                gug_ref[f0 : f0 + size, pl.ds(c0, TILE)] = mm(
                    xin[:, f0 : f0 + size], hb[:, pl.ds(c0 + HID, TILE)], TN
                ).astype(BF16)

    def down_grads():
        @pl.loop(0, HID // 256)
        def _(n):
            c0 = pl.multiple_of(n * 256, 256)
            dg_ref[pl.ds(c0, 256), :] = mm(hb[:, pl.ds(c0, 256)], din[...], TN).astype(BF16)

    down_grads()
    many(backo, (HALF - 1) * 2 * CAP, reto_s, reto_r).wait_recv()
    for c0 in (0, CAP):
        total = jnp.zeros((CAP, FEAT), F32)
        for n in range(HALF):
            total = total + backo[n * 2 * CAP + c0 : n * 2 * CAP + c0 + CAP, :].astype(F32)
        if c0:
            zsend[...] = total.astype(BF16)
        else:
            ovx_total = total
    back_z = remote(zsend, zrecv, retz_s, retz_r, z_partner)
    back_z.start()
    gate_up_grads()
    many(back, BASE - CAP, ret_s, ret_r).wait_recv()
    back_z.wait_recv()
    over_rows = (ovx_total + zrecv[...].astype(F32)).astype(BF16)
    over_at = picks(0.0, CAP, slots[1:2, :])
    total = mm(over_at, over_rows, TN)
    for b in range(BASE // 128):
        pick = picks(128.0 * b, 128, slots[0:1, :])
        total = total + mm(pick, back[b * 128 : (b + 1) * 128, :], TN)
    tg_ref[...] = total.astype(BF16)

    for copy in ovz:
        copy.wait_send()
    for n in range(2):
        many(sendx, BASE - CAP, base_send.at[n], base_recv.at[n]).wait_send()
        many(xin, (HALF - 1) * 2 * CAP, ov_send.at[n], ov_recv.at[n]).wait_send()
    many(rowg, BASE - CAP, ret_s, ret_r).wait_send()
    many(rowg, (HALF - 1) * 2 * CAP, reto_s, reto_r).wait_send()
    back_z.wait_send()
    for k in range(CHUNKS):
        core_copy(k).wait_send()
        for d in range(4):

            @pl.when(z < d)
            def _():
                rs_copy(k, 0, d).wait_send()

            @pl.when(z > d)
            def _():
                rs_copy(k, 1, d).wait_send()

            @pl.when(jnp.logical_and(z >= d, z < 3))
            def _():
                ag_copy(k, 0, d).wait_send()

            @pl.when(jnp.logical_and(z <= d, z > 0))
            def _():
                ag_copy(k, 1, d).wait_send()

            ag_copy(k, 2, d).wait_send()


def local(tokens, d_out, row_expert, w_gate_up, w_down):
    vmem = pl.BlockSpec(memory_space=pltpu.VMEM)
    hbm = pl.BlockSpec(memory_space=pl.ANY)
    dma = pltpu.SemaphoreType.DMA

    def buf(count, width, kind=BF16):
        return pltpu.VMEM((count, width), kind)

    token_grads, gate_up_grads, down_grads = pl.pallas_call(
        kernel,
        out_shape=(
            jax.ShapeDtypeStruct((ROWS, FEAT), BF16),
            jax.ShapeDtypeStruct((FEAT, 2 * HID), BF16),
            jax.ShapeDtypeStruct((HID, FEAT), BF16),
        ),
        in_specs=[vmem, vmem, vmem, hbm, hbm],
        out_specs=(vmem, vmem, vmem),
        scratch_shapes=[
            buf(FEAT, 2 * HID), buf(HID, FEAT),
            buf(SLOTS, FEAT), buf(SLOTS, FEAT),
            buf(BASE, FEAT), buf(BASE, FEAT),
            buf(2 * CAP, FEAT), buf(2 * CAP, FEAT),
            buf(SLOTS // 2, WIDE), buf(SLOTS // 2, WIDE),
            buf(SLOTS // 2, WIDE, F32),
            buf(CHUNKS * 8 * UNIT, WIDE), buf(CHUNKS * 8 * UNIT, WIDE),
            buf(SLOTS, WIDE),
            buf(SLOTS, FEAT), buf(BASE, FEAT), buf(BASE, FEAT),
            buf(CAP, FEAT), buf(CAP, FEAT),
            buf(8, ROWS, F32), buf(16, FEAT),
            dma((2,)), dma((2,)), dma((2,)), dma((2,)), dma((2,)), dma((2,)), dma((2,)),
            dma((CHUNKS,)), dma((CHUNKS,)),
            dma((CHUNKS, 2, 4)), dma((CHUNKS, 2, 4)),
            dma((CHUNKS, 3, 4)), dma((CHUNKS, 2, 4)),
            dma, dma, dma, dma, dma, dma,
        ],
        compiler_params=pltpu.CompilerParams(
            collective_id=0, has_side_effects=True, vmem_limit_bytes=62 * 1024 * 1024
        ),
        cost_estimate=pl.CostEstimate(flops=15_000_000_000, bytes_accessed=14_000_000, transcendentals=131072),
        name="expert_backward",
    )(
        row_expert.reshape(1, ROWS), tokens, d_out,
        w_gate_up.reshape(FEAT, 2 * HID), w_down.reshape(HID, FEAT),
    )
    return (
        token_grads,
        gate_up_grads.reshape(1, FEAT, 2, HID),
        down_grads.reshape(1, HID, FEAT),
    )


def solution(mesh):
    return jax.shard_map(
        local,
        mesh=mesh,
        in_specs=(
            P("exp", "grp"),
            P("exp", "grp"),
            P("exp"),
            P("exp", "grp", None, None),
            P("exp", None, "grp"),
        ),
        out_specs=(P("exp", "grp"), P("exp", "grp", None, None), P("exp", None, "grp")),
        check_vma=False,
    )
```

time: 356 us -> 219 us (0.62); the launches traced: 349 us -> 219 us
  waiting for transfers between devices: 233 us -> 0 us
  Pallas kernels: 0 us -> 204 us
  matrix products: 36.2 us -> 0 us
  starting transfers between devices: 31.5 us -> 0 us
  between operations: 14.1 us -> 0.66 us
  local copies, waits for them, and re-layouts: 25.8 us -> 14.4 us
  other arithmetic: 8.9 us -> 0 us
    pallas_call x0 -> x1, Pallas kernels: none -> 204 us  [local(): pl.pallas_call(kernel, out_shape=(jax.ShapeDtypeStruct((ROWS, FEAT), BF16...]
    psum x1 -> x0, waiting for transfers between devices: 156 us -> none  [local(): lax.psum(hidden_part.astype(jnp.bfloat16), 'grp').astype(jnp.float32)]
    all_to_all x3 -> x0, waiting for transfers between devices: 77.1 us -> none  [the longest x1 40.7 us: local(): lax.all_to_all(place_rows(d_out, slot_index, slot_total).reshape(expert_c...]
    dot_general x5 -> x0, matrix products: 36.2 us -> none  [the longest x1 9.06 us: partial_products(): jnp.dot(rows_in, local_gate_up, preferred_element_type=jnp.float32)]
    all_to_all x3 -> x0, starting transfers between devices: 31.3 us -> none  [the longest x1 14 us: local(): lax.all_to_all(place_rows(d_out, slot_index, slot_total).reshape(expert_c...]
    scatter x2 -> x0, local copies, waits for them, and re-layouts: 7.14 us -> none  [place_rows(): return blank_rows.at[slot_index].set(source_rows, mode='drop')]
    convert_element_type x2 -> x0, other arithmetic: 4.22 us -> none  [the longest x1 3.4 us: local(): lax.psum(gate_part.astype(jnp.bfloat16), 'grp').astype(jnp.float32)]
    gather x1 -> x0, local copies, waits for them, and re-layouts: 3.98 us -> none  [local(): token_grads = returned.reshape(slot_total, feature_share)[slot_index]]
  transfers between devices with their start and end apart: 4 -> 0, of which waited for: 4 -> 0; matrix products, arithmetic and copies ran while one was open for 11% -> 0% of each run, Pallas kernels for 0% -> 0%
where the time goes in v1:
time: 219 us
  Pallas kernels  204 us (93%)
  local copies, waits for them, and re-layouts  14.4 us (7%)
    pallas_call x1, Pallas kernels, local(): pl.pallas_call(kernel, out_shape=(jax.ShapeDtypeStruct((ROWS, FEAT), BF16...  204 us
    reshape x1, local copies, waits for them, and re-layouts, local(): gate_up_grads.reshape(1, FEAT, 2, HID)  7.3 us
    unnamed x7, local copies, waits for them, and re-layouts  7.11 us

profile of v1, /device:TPU:24, one launch (start us, length us, event | category | flops | bytes accessed | tf_op | source)
XLA Modules:
  0.0 219.1 jit_solution(5646613465627382328)
XLA Ops:
  0.6 5.1 %copy.8 = bf16[112,8,2,1024]{3,1,2,0:T(8,128)(2,1)} copy(bf16[112,8,2,1024]{3,2,1,0:T(2,128)(2,1)} %bitcast.6) | data formatting | bytes 7340032
  5.7 204.0 %expert_backward.1 = (bf16[256,896]{1,0:T(8,128)(2,1)}, bf16[896,2048]{1,0:T(8,128)(2,1)}, bf16[1024,896]{1,0:T(8,128)(2,1)}) custom-call(s32[1,256]{1,0:T(1,128)} %bitcast.10, bf16[256,896]{1,0:T(8,128)(2,1)} %tok_ref.1, bf16[256,896]{1,0:T(8,128)(2,1)} %dout_ref.1, bf16[896,2048]{1,0:T(8,128)(2,1)} %bitcast.7, bf16[1024,896]{1,0:T(8,128)(2,1)} %bitcast.9), custom_call_target="tpu_custom_call" | custom-call | flops 15000000512 | bytes 14000000 | tf_op jit(solution)/shard_map/expert_backward/pallas_call | solution.py:477
  209.8 0.0 copy-start.1
  209.8 0.0 copy-start
  209.8 7.3 %reshape.24 = bf16[1,896,2,1024]{3,2,1,0:T(2,128)(2,1)} reshape(bf16[896,2048]{1,0:T(8,128)(2,1)} %get-tuple-element.7) | data formatting | bytes 7340032 | tf_op jit(solution)/shard_map/reshape | solution.py:515
  217.1 0.0 copy-done.1
  217.1 0.8 copy.11
  217.9 0.0 copy-done
  217.9 1.2 copy.12
Async XLA Ops:
  209.8 7.3 %copy-start.1 = (bf16[256,896]{1,0:T(8,128)(2,1)S(1)}, bf16[256,896]{1,0:T(8,128)(2,1)}, u32[]{:S(2)}) copy-start(bf16[256,896]{1,0:T(8,128)(2,1)} %get-tuple-element.12) | copy-start | bytes 1376260
  209.8 8.1 %copy-start = (bf16[1024,896]{1,0:T(8,128)(2,1)S(1)}, bf16[1024,896]{1,0:T(8,128)(2,1)}, u32[]{:S(2)}) copy-start(bf16[1024,896]{1,0:T(8,128)(2,1)} %get-tuple-element.8) | copy-start | bytes 5505028

commit v2 on v1

v2 whole, which is shorter than its diff:
```python
import jax
import jax.numpy as jnp
from jax import lax
from jax.experimental import pallas as pl
from jax.experimental.pallas import tpu as pltpu
from jax.sharding import PartitionSpec as P

MESH = pl.DeviceIdType.MESH
F32 = jnp.float32
BF16 = jnp.bfloat16

ROWS = 256
FEAT = 896
HID = 1024
WIDE = 3 * HID
N_EXP = 32
HALF = 16
CAP = 16
BASE = N_EXP * CAP
SLOTS = 2 * BASE
GROUPS = 4
CHUNK = BASE // GROUPS
SHARE = CHUNK // 2
QUARTER = 64
UNIT = 16
TILE = 512
RINGS = 6

NN = (((1,), (0,)), ((), ()))
NT = (((1,), (1,)), ((), ()))
TN = (((0,), (0,)), ((), ()))


def mm(a, b, dims=NN):
    return lax.dot_general(a, b, dims, preferred_element_type=F32)


def rows(start, size):
    return pl.ds(pl.multiple_of(start, 16), size)


def kernel(
    expert_ref, tok_ref, dout_ref, wgu_hbm, wd_hbm,
    tg_ref, gug_hbm, dg_hbm,
    paired, down, wgu, wd, xin, din, sendx, sendd, ovx, ovd,
    csend, crecv, acc, rs_send, rs_recv, hb,
    ocsend, ocrecv, oacc, oxsend, oxrecv, ors_send, ors_recv, hbo,
    rowg, back, backo, zsend, zrecv, slots, hotm,
    w_sem, o_sem, base_send, base_recv, ovz_send, ovz_recv, ov_send, ov_recv,
    c_send, c_recv, x_send, x_recv, y_send, y_recv, yc_send, yc_recv,
    rs_s, rs_r, ag_s, ag_r, ret_s, ret_r, reto_s, reto_r, retz_s, retz_r,
):
    me_e = lax.axis_index("exp")
    me_g = lax.axis_index("grp")
    z = me_g // 2
    core = lax.rem(me_g, 2)
    half = me_e // HALF
    q = lax.rem(me_e, HALF)
    z_partner = {"exp": lax.rem(me_e + HALF, N_EXP)}
    core_partner = {"grp": me_g + 1 - 2 * core}
    x = lax.rem(me_e, 4)
    to_right = {"grp": lax.rem(me_g + 2, 8)}
    to_left = {"grp": lax.rem(me_g + 6, 8)}

    def remote(src, dst, s_sem, r_sem, dev):
        return pltpu.make_async_remote_copy(
            src_ref=src, dst_ref=dst, send_sem=s_sem, recv_sem=r_sem, device_id=dev, device_id_type=MESH
        )

    def peer(p, way):
        side = lax.rem(p // 4, 2)
        return lax.rem(half + side, 2) * HALF + lax.rem(q + HALF + way * ((p // 8) * 4 + lax.rem(p, 4)), HALF)

    w1 = pltpu.make_async_copy(wgu_hbm, paired, w_sem.at[0])
    w2 = pltpu.make_async_copy(wd_hbm, wd, w_sem.at[1])
    w1.start()
    w2.start()
    barrier = pltpu.get_barrier_semaphore()

    @pl.loop(1, N_EXP)
    def _(p):
        pl.semaphore_signal(
            barrier, inc=1, device_id={"exp": lax.rem(me_e + p, N_EXP)}, device_id_type=MESH
        )

    @pl.loop(1, 8)
    def _(p):
        pl.semaphore_signal(barrier, inc=1, device_id={"grp": lax.rem(me_g + p, 8)}, device_id_type=MESH)

    expert = expert_ref[...]
    e_iota = lax.broadcasted_iota(jnp.int32, (N_EXP, ROWS), 0)
    mine = (expert == e_iota).astype(F32)
    upto = (
        lax.broadcasted_iota(jnp.int32, (ROWS, ROWS), 0) <= lax.broadcasted_iota(jnp.int32, (ROWS, ROWS), 1)
    ).astype(F32).astype(BF16)
    running = mm(mine.astype(BF16), upto)
    rank = jnp.sum(running * mine, axis=0, keepdims=True) - 1.0
    slot = jnp.where(rank < CAP, expert.astype(F32) * CAP + rank, -1.0)
    over = rank - CAP
    slots[0:1, :] = slot
    slots[1:2, :] = over
    loads = jnp.sum(mine, axis=1, keepdims=True)
    is_me = (lax.broadcasted_iota(jnp.int32, (N_EXP, 1), 0) == me_e).astype(F32)
    hot = jnp.sum(jnp.where(loads > CAP + 0.5, 1.0, 0.0) * is_me, axis=0, keepdims=True)
    hotm[...] = jnp.broadcast_to(hot, (16, FEAT)).astype(BF16)

    def picks(start, size, values):
        at = lax.broadcasted_iota(jnp.int32, (size, ROWS), 0).astype(F32) + start
        return (at == values).astype(F32).astype(BF16)

    over_pick = picks(0.0, CAP, over)
    base_pick = picks(0.0, BASE, slot)
    for src, base, further in ((tok_ref, sendx, ovx), (dout_ref, sendd, ovd)):
        for c0, size in ((0, 256), (256, 256), (512, 256), (768, 128)):
            col = slice(c0, c0 + size)
            base[:, col] = mm(base_pick, src[:, col]).astype(BF16)
            further[0:CAP, col] = mm(over_pick, src[:, col]).astype(BF16)
    pl.semaphore_wait(barrier, N_EXP - 1 + 7)

    ovz = [
        remote(buf.at[pl.ds(0, CAP)], buf.at[pl.ds(CAP, CAP)], ovz_send.at[n], ovz_recv.at[n], z_partner)
        for n, buf in enumerate((ovx, ovd))
    ]
    for copy in ovz:
        copy.start()
    over_place = BASE + q * 2 * CAP

    def many(buf, count, s_sem, r_sem):
        part = buf.at[pl.ds(0, count)]
        return remote(part, part, s_sem, r_sem, z_partner)

    def base_block(k, p):
        to = peer(p, 1)
        for n, (src, dst) in enumerate(((sendx, xin), (sendd, din))):
            remote(
                src.at[rows(to * CAP, CAP)], dst.at[rows(p * CAP, CAP)],
                base_send.at[n, k], base_recv.at[n, k], {"exp": to},
            ).start()

    def further_block(first, p):
        to = half * HALF + lax.rem(q + p, HALF)
        for n, (src, dst) in enumerate(((ovx, xin), (ovd, din))):
            remote(
                src.at[pl.ds(first, CAP)], dst.at[rows(over_place + first, CAP)],
                ov_send.at[n], ov_recv.at[n], {"exp": to},
            ).start()

    def stage_d(k):
        @pl.loop(0, 8)
        def _(n):
            p = k * 8 + lax.rem(n + 4, 8)
            if k:
                base_block(k, p)
            else:

                @pl.when(p > 0)
                def _():
                    base_block(k, p)

            if k < 2:

                @pl.when(n > 0)
                def _():
                    further_block(k * CAP, 2 * n)

                further_block(k * CAP, 2 * n + 1)

    def left(k):
        for n, buf in enumerate((sendx, sendd)):
            many(buf, (8 if k else 7) * CAP, base_send.at[n, k], base_recv.at[n, k]).wait_send()

    stage_d(0)
    xin[0:CAP, :] = sendx[rows(me_e * CAP, CAP), :]
    din[0:CAP, :] = sendd[rows(me_e * CAP, CAP), :]
    w1.wait()

    @pl.loop(0, FEAT // 16)
    def _(n):
        at = rows(n * 16, 16)
        wgu[at, 0:HID] = paired[0, at, 0, :]
        wgu[at, HID:] = paired[0, at, 1, :]

    w2.wait()
    for copy in ovz:
        copy.wait_recv()
    stage_d(1)
    xin[rows(over_place, 2 * CAP), :] = ovx[...]
    din[rows(over_place, 2 * CAP), :] = ovd[...]

    def base_rows(k):
        for n, buf in enumerate((xin, din)):
            many(buf, (8 if k else 7) * CAP, base_send.at[n, k], base_recv.at[n, k]).wait_recv()

    def core_copy(n):
        src, dst = (csend, crecv) if n < GROUPS else (ocsend, ocrecv)
        part = pl.ds(n * SHARE, SHARE) if n < GROUPS else pl.ds((n - GROUPS) * 4 * QUARTER, 4 * QUARTER)
        return remote(src.at[part], dst.at[part], c_send.at[n], c_recv.at[n], core_partner)

    def stage_p(k):
        here = pl.ds(k * CHUNK, CHUNK)

        @pl.loop(0, 2 * HID // TILE)
        def _(n):
            col = pl.ds(pl.multiple_of(n * TILE, TILE), TILE)
            acc[here, col] = mm(xin[here, :], wgu[:, col])

        @pl.loop(0, HID // TILE)
        def _(n):
            col = pl.ds(pl.multiple_of(2 * HID + n * TILE, TILE), TILE)
            acc[here, col] = mm(din[here, :], wd[rows(n * TILE, TILE), :], NT)

        @pl.loop(0, SHARE // 16)
        def _(n):
            theirs = rows(k * CHUNK + (1 - core) * SHARE + n * 16, 16)
            csend[rows(k * SHARE + n * 16, 16), :] = acc[theirs, :].astype(BF16)

        core_copy(k).start()

    def stage_c(k):
        core_copy(k).wait_recv()

        @pl.loop(0, SHARE // 16)
        def _(n):
            mine = rows(k * CHUNK + core * SHARE + n * 16, 16)
            acc[mine, :] += crecv[rows(k * SHARE + n * 16, 16), :].astype(F32)

    def stage_po(h):
        @pl.loop(0, BASE // 128)
        def _(n):
            rows_in = xin[rows(BASE + n * 128, 128), :]
            grads_in = din[rows(BASE + n * 128, 128), :]
            here = rows(h * BASE + n * 128, 128)
            oacc[here, 0:TILE] = mm(rows_in, wgu[:, h * TILE : (h + 1) * TILE])
            oacc[here, TILE : 2 * TILE] = mm(rows_in, wgu[:, HID + h * TILE : HID + (h + 1) * TILE])
            oacc[here, 2 * TILE :] = mm(grads_in, wd[h * TILE : (h + 1) * TILE, :], NT)

        @pl.loop(0, 4 * QUARTER // 16)
        def _(n):
            theirs = rows(h * BASE + (1 - core) * 4 * QUARTER + n * 16, 16)
            ocsend[rows(h * 4 * QUARTER + n * 16, 16), :] = oacc[theirs, :].astype(BF16)

        core_copy(GROUPS + h).start()

    y = q // 4
    spot = (x, y)

    def along(h, p):
        return {"exp": me_e - x + lax.rem(x + p, 4) if h == 0 else me_e - 4 * y + 4 * lax.rem(y + p, 4)}

    def x_copy(h, p):
        return remote(
            oxsend.at[rows(h * 4 * QUARTER + lax.rem(spot[h] + p, 4) * QUARTER, QUARTER)],
            oxrecv.at[pl.ds((h * 3 + p - 1) * QUARTER, QUARTER)],
            x_send.at[h, p - 1], x_recv.at[h, p - 1], along(h, p),
        )

    def stage_co(h):
        core_copy(GROUPS + h).wait_recv()

        @pl.loop(0, 4 * QUARTER // 16)
        def _(n):
            mine = rows(h * BASE + core * 4 * QUARTER + n * 16, 16)
            here = rows(h * 4 * QUARTER + n * 16, 16)
            value = oacc[mine, :] + ocrecv[here, :].astype(F32)
            oacc[mine, :] = value
            oxsend[here, :] = value.astype(BF16)

        for p in (1, 2, 3):
            x_copy(h, p).start()

    def stage_xo(h):
        for p in (1, 2, 3):
            x_copy(h, p).wait_recv()

        @pl.loop(0, QUARTER // 16)
        def _(n):
            at = rows(h * BASE + further_row(spot[h], core) + n * 16, 16)
            value = oacc[at, :]
            for p in range(3):
                value = value + oxrecv[rows((h * 3 + p) * QUARTER + n * 16, 16), :].astype(F32)
            oacc[at, :] = value

    def ring(r):
        if r < GROUPS:
            return acc, rs_send, rs_recv, hb, r * 6, HID
        return oacc, ors_send, ors_recv, hbo, (r - GROUPS) * 6, TILE

    def block_row(r, c, j):
        if r < GROUPS:
            return r * CHUNK + c * SHARE + j * UNIT
        return (r - GROUPS) * BASE + further_row(spot[r - GROUPS], c) + j * UNIT

    def further_row(at, c):
        return c * 4 * QUARTER + at * QUARTER

    def rs_copy(r, way, d):
        _, send, recv, _, first, _ = ring(r)
        part = rows((first + way * 3 + d - 1 + way) * UNIT, UNIT)
        return remote(send.at[part], recv.at[part], rs_s.at[r, way, d], rs_r.at[r, way, d], (to_right, to_left)[way])

    def rs_forward(r, way, d, start):
        total, send, recv, _, first, _ = ring(r)
        part = pl.ds((first + way * 3 + d - 1 + way) * UNIT, UNIT)
        copy = rs_copy(r, way, d)
        value = total[rows(block_row(r, core, d), UNIT), :]
        if not start:
            copy.wait_recv()
            value = value + recv[part, :].astype(F32)
        send[part, :] = value.astype(BF16)
        copy.start()

    def stage_e(r):
        @pl.when(z == 0)
        def _():
            for d in (3, 2, 1):
                rs_forward(r, 0, d, True)

        @pl.when(z == 3)
        def _():
            for d in (0, 1, 2):
                rs_forward(r, 1, d, True)

    def stage_m1(r):
        @pl.when(z == 1)
        def _():
            rs_forward(r, 0, 3, False)

        @pl.when(z == 2)
        def _():
            rs_forward(r, 1, 0, False)

    def stage_m2(r):
        @pl.when(z == 1)
        def _():
            rs_forward(r, 0, 2, False)
            rs_forward(r, 1, 0, False)

        @pl.when(z == 2)
        def _():
            rs_forward(r, 1, 1, False)
            rs_forward(r, 0, 3, False)

    def ag_copy(r, way, j):
        out = ring(r)[3]
        part = rows(block_row(r, core, j), UNIT)
        return remote(
            out.at[part], out.at[part], ag_s.at[r, way, j], ag_r.at[r, core, j], (to_right, to_left, core_partner)[way]
        )

    def stage_f(r):
        total, _, recv, out, first, wide = ring(r)
        at = rows(block_row(r, core, z), UNIT)

        def fold(way):
            rs_copy(r, way, z).wait_recv()
            total[at, :] += recv[rows((first + way * 3 + z - 1 + way) * UNIT, UNIT), :].astype(F32)

        @pl.when(z > 0)
        def _():
            fold(0)

        @pl.when(z < 3)
        def _():
            fold(1)

        @pl.loop(0, wide // 256)
        def _(n):
            c0 = pl.multiple_of(n * 256, 256)
            gate = total[at, pl.ds(c0, 256)]
            up = total[at, pl.ds(c0 + wide, 256)]
            grad = total[at, pl.ds(c0 + 2 * wide, 256)]
            sig = jax.nn.sigmoid(gate)
            act = gate * sig
            slope = sig * (1.0 + gate * (1.0 - sig))
            out[at, pl.ds(c0, 256)] = (act * up).astype(BF16)
            out[at, pl.ds(c0 + wide, 256)] = (grad * up * slope).astype(BF16)
            out[at, pl.ds(c0 + 2 * wide, 256)] = (grad * act).astype(BF16)

        @pl.when(z < 3)
        def _():
            ag_copy(r, 0, z).start()

        @pl.when(z > 0)
        def _():
            ag_copy(r, 1, z).start()

        ag_copy(r, 2, z).start()

    def stage_a(r, dist):
        from_left = z - dist
        from_right = z + dist

        @pl.when(from_left >= 0)
        def _():
            ag_copy(r, 0, from_left).wait_recv()

            @pl.when(z < 3)
            def _():
                ag_copy(r, 0, from_left).start()

            ag_copy(r, 2, from_left).start()

        @pl.when(from_right <= 3)
        def _():
            ag_copy(r, 1, from_right).wait_recv()

            @pl.when(z > 0)
            def _():
                ag_copy(r, 1, from_right).start()

            ag_copy(r, 2, from_right).start()

    def y_copy(h, p):
        part = rows(h * BASE + further_row(spot[h], core), QUARTER)
        return remote(hbo.at[part], hbo.at[part], y_send.at[h, p - 1], y_recv.at[h, p - 1], along(h, p))

    def yc_copy(h, p, c):
        part = rows(h * BASE + further_row(lax.rem(spot[h] + 4 - p, 4), c), QUARTER)
        return remote(hbo.at[part], hbo.at[part], yc_send.at[h, p - 1], yc_recv.at[h, p - 1], core_partner)

    def stage_z(h):
        for p in (1, 2, 3):
            y_copy(h, p).start()

    def stage_y(h):
        for p in (1, 2, 3):
            y_copy(h, p).wait_recv()
            yc_copy(h, p, core).start()

    def from_core(r):
        out = ring(r)[3]
        for j in range(4):
            part = rows(block_row(r, 1 - core, j), UNIT)
            remote(
                out.at[part], out.at[part], ag_s.at[r, 2, j], ag_r.at[r, 1 - core, j], core_partner
            ).wait_recv()

    def stage_g(k):
        from_core(k)
        here = pl.ds(k * CHUNK, CHUNK)
        for c0, size in ((0, 256), (256, 256), (512, 256), (768, 128)):
            rowg[here, c0 : c0 + size] = mm(hb[here, HID:], wgu[c0 : c0 + size, :], NT).astype(BF16)

        @pl.loop(k * 8 if k else 1, k * 8 + 8)
        def _(p):
            to = peer(p, -1)
            remote(
                rowg.at[rows(p * CAP, CAP)], back.at[rows(me_e * CAP, CAP)], ret_s, ret_r, {"exp": to}
            ).start()

        if k == 0:
            back[rows(me_e * CAP, CAP), :] = rowg[0:CAP, :]

    def stage_go():
        for h in range(2):
            from_core(GROUPS + h)
            for p in (1, 2, 3):
                yc_copy(h, p, 1 - core).wait_recv()

        @pl.loop(0, 2)
        def _(n):
            for c0, size in ((0, 256), (256, 256), (512, 256), (768, 128)):
                value = jnp.zeros((256, size), F32)
                for h in range(2):
                    for b in range(2):
                        value = value + mm(
                            hbo[rows(h * BASE + n * 256, 256), (1 + b) * TILE : (2 + b) * TILE],
                            wgu[c0 : c0 + size, b * HID + h * TILE : b * HID + (h + 1) * TILE], NT,
                        )
                value = value * hotm[0:1, c0 : c0 + size].astype(F32)
                rowg[rows(BASE + n * 256, 256), c0 : c0 + size] = value.astype(BF16)

            @pl.loop(0, 8)
            def _(p):
                near = n * 8 + lax.rem(q + p, 8)

                @pl.when(near != q)
                def _():
                    remote(
                        rowg.at[rows(BASE + near * 2 * CAP, 2 * CAP)], backo.at[rows(q * 2 * CAP, 2 * CAP)],
                        reto_s, reto_r, {"exp": half * HALF + near},
                    ).start()

        backo[rows(q * 2 * CAP, 2 * CAP), :] = rowg[rows(BASE + q * 2 * CAP, 2 * CAP), :]

    def hot_rows():
        many(xin, (HALF - 1) * 2 * CAP, ov_send.at[0], ov_recv.at[0]).wait_recv()
        many(din, (HALF - 1) * 2 * CAP, ov_send.at[1], ov_recv.at[1]).wait_recv()

        @pl.loop(0, BASE // 16)
        def _(n):
            at = rows(BASE + n * 16, 16)
            xin[at, :] = xin[at, :] * hotm[...]
            din[at, :] = din[at, :] * hotm[...]

    left(0)
    stage_d(2)
    base_rows(0)
    stage_p(0)
    left(1)
    stage_d(3)
    base_rows(1)
    stage_p(1)
    hot_rows()
    stage_po(0)
    stage_po(1)
    stage_c(0)
    stage_e(0)
    stage_c(1)
    stage_e(1)
    stage_co(0)
    stage_co(1)
    stage_m1(0)
    stage_m1(1)
    stage_m2(0)
    stage_m2(1)
    stage_f(0)
    stage_f(1)
    base_rows(2)
    stage_p(2)
    stage_c(2)
    stage_xo(0)
    stage_xo(1)
    stage_e(4)
    stage_e(5)
    stage_a(0, 1)
    stage_a(1, 1)
    stage_m1(4)
    stage_m1(5)
    stage_a(0, 2)
    stage_a(1, 2)
    stage_m2(4)
    stage_m2(5)
    stage_a(0, 3)
    stage_a(1, 3)
    stage_f(4)
    stage_f(5)
    base_rows(3)
    stage_p(3)
    stage_c(3)
    stage_e(2)
    stage_e(3)
    stage_a(4, 1)
    stage_a(5, 1)
    stage_m1(2)
    stage_m1(3)
    stage_a(4, 2)
    stage_a(5, 2)
    stage_m2(2)
    stage_m2(3)
    stage_a(4, 3)
    stage_z(0)
    stage_a(5, 3)
    stage_z(1)
    stage_f(2)
    stage_f(3)
    stage_g(0)
    stage_g(1)
    stage_a(2, 1)
    stage_a(3, 1)
    stage_a(2, 2)
    stage_a(3, 2)
    stage_a(2, 3)
    stage_a(3, 3)
    stage_y(0)
    stage_y(1)
    stage_go()
    stage_g(2)
    stage_g(3)

    def gate_up_grads():
        for b in range(2):

            @pl.loop(0, HID // TILE)
            def _(n):
                c0 = pl.multiple_of(n * TILE, TILE)
                near = hb[:, pl.ds(c0 + HID * (1 + b), TILE)]
                further = hbo[rows(n * BASE, BASE), (1 + b) * TILE : (2 + b) * TILE]
                for f0, size in ((0, 256), (256, 256), (512, 256), (768, 128)):
                    value = mm(xin[0:BASE, f0 : f0 + size], near, TN)
                    value = value + mm(xin[BASE:, f0 : f0 + size], further, TN)
                    paired[0, f0 : f0 + size, b, pl.ds(c0, TILE)] = value.astype(BF16)

    def down_grads():
        for h in range(2):

            @pl.loop(0, 2)
            def _(n):
                c0 = pl.multiple_of(n * 256, 256)
                value = mm(hb[:, pl.ds(c0 + h * TILE, 256)], din[0:BASE, :], TN)
                value = value + mm(hbo[h * BASE : (h + 1) * BASE, pl.ds(c0, 256)], din[BASE:, :], TN)
                down[pl.ds(c0 + h * TILE, 256), :] = value.astype(BF16)

    out_down = pltpu.make_async_copy(down, dg_hbm, o_sem.at[0])
    out_gate_up = pltpu.make_async_copy(paired, gug_hbm, o_sem.at[1])
    gate_up_grads()
    out_gate_up.start()
    many(backo, (HALF - 1) * 2 * CAP, reto_s, reto_r).wait_recv()
    for c0 in (0, CAP):
        total = jnp.zeros((CAP, FEAT), F32)
        for n in range(HALF):
            total = total + backo[n * 2 * CAP + c0 : n * 2 * CAP + c0 + CAP, :].astype(F32)
        if c0:
            zsend[...] = total.astype(BF16)
        else:
            ovx_total = total
    back_z = remote(zsend, zrecv, retz_s, retz_r, z_partner)
    back_z.start()
    down_grads()
    out_down.start()
    many(back, BASE - CAP, ret_s, ret_r).wait_recv()
    back_z.wait_recv()
    over_rows = (ovx_total + zrecv[...].astype(F32)).astype(BF16)
    over_at = picks(0.0, CAP, slots[1:2, :])
    total = mm(over_at, over_rows, TN)
    for b in range(BASE // 128):
        pick = picks(128.0 * b, 128, slots[0:1, :])
        total = total + mm(pick, back[b * 128 : (b + 1) * 128, :], TN)
    tg_ref[...] = total.astype(BF16)

    out_down.wait()
    out_gate_up.wait()
    for copy in ovz:
        copy.wait_send()
    left(2)
    left(3)
    for n in range(2):
        many(xin, (HALF - 1) * 2 * CAP, ov_send.at[n], ov_recv.at[n]).wait_send()
    many(rowg, BASE - CAP, ret_s, ret_r).wait_send()
    many(rowg, (HALF - 1) * 2 * CAP, reto_s, reto_r).wait_send()
    back_z.wait_send()
    for n in range(RINGS):
        core_copy(n).wait_send()
    for h in range(2):
        for p in (1, 2, 3):
            x_copy(h, p).wait_send()
            y_copy(h, p).wait_send()
            yc_copy(h, p, core).wait_send()
    for r in range(RINGS):
        for d in range(4):
            if d > 0:

                @pl.when(z < d)
                def _():
                    rs_copy(r, 0, d).wait_send()

            if d < 3:

                @pl.when(z > d)
                def _():
                    rs_copy(r, 1, d).wait_send()

            @pl.when(jnp.logical_and(z >= d, z < 3))
            def _():
                ag_copy(r, 0, d).wait_send()

            @pl.when(jnp.logical_and(z <= d, z > 0))
            def _():
                ag_copy(r, 1, d).wait_send()

            ag_copy(r, 2, d).wait_send()


def hand_over(tg, gug, dg, tg_out, gug_out, dg_out, tg_via, gug_via, dg_via, sems):
    parts = [(tg, tg_via, tg_out)]
    for n in range(2):
        part = pl.ds(n * (HID // 2), HID // 2)
        parts.append((dg.at[part], dg_via.at[part], dg_out.at[part]))
    for n in range(4):
        part = pl.ds(n * (FEAT // 4), FEAT // 4)
        parts.append((gug.at[0, part], gug_via.at[0, part], gug_out.at[0, part]))
    here = [pltpu.make_async_copy(a, b, sems.at[0, n]) for n, (a, b, _) in enumerate(parts)]
    there = [pltpu.make_async_copy(b, c, sems.at[1, n]) for n, (_, b, c) in enumerate(parts)]
    for copy in here:
        copy.start()
    for first, then in zip(here, there):
        first.wait()
        then.start()
    for copy in there:
        copy.wait()


def local(tokens, d_out, row_expert, w_gate_up, w_down):
    vmem = pl.BlockSpec(memory_space=pltpu.VMEM)
    hbm = pl.BlockSpec(memory_space=pl.ANY)
    dma = pltpu.SemaphoreType.DMA

    def buf(count, width, kind=BF16):
        return pltpu.VMEM((count, width), kind)

    token_grads, gate_up_grads, down_grads = pl.pallas_call(
        kernel,
        out_shape=(
            jax.ShapeDtypeStruct((ROWS, FEAT), BF16),
            jax.ShapeDtypeStruct((1, FEAT, 2, HID), BF16),
            jax.ShapeDtypeStruct((HID, FEAT), BF16),
        ),
        in_specs=[vmem, vmem, vmem, hbm, hbm],
        out_specs=(vmem, hbm, hbm),
        scratch_shapes=[
            pltpu.VMEM((1, FEAT, 2, HID), BF16), buf(HID, FEAT),
            buf(FEAT, 2 * HID), buf(HID, FEAT),
            buf(SLOTS, FEAT), buf(SLOTS, FEAT),
            buf(BASE, FEAT), buf(BASE, FEAT),
            buf(2 * CAP, FEAT), buf(2 * CAP, FEAT),
            buf(BASE // 2, WIDE), buf(BASE // 2, WIDE),
            buf(BASE, WIDE, F32),
            buf(GROUPS * 6 * UNIT, WIDE), buf(GROUPS * 6 * UNIT, WIDE),
            buf(BASE, WIDE),
            buf(8 * QUARTER, 3 * TILE), buf(8 * QUARTER, 3 * TILE),
            buf(2 * BASE, 3 * TILE, F32),
            buf(8 * QUARTER, 3 * TILE), buf(6 * QUARTER, 3 * TILE),
            buf(2 * 6 * UNIT, 3 * TILE), buf(2 * 6 * UNIT, 3 * TILE),
            buf(2 * BASE, 3 * TILE),
            buf(SLOTS, FEAT), buf(BASE, FEAT), buf(BASE, FEAT),
            buf(CAP, FEAT), buf(CAP, FEAT),
            buf(8, ROWS, F32), buf(16, FEAT),
            dma((2,)), dma((2,)), dma((2, GROUPS)), dma((2, GROUPS)), dma((2,)), dma((2,)), dma((2,)), dma((2,)),
            dma((RINGS,)), dma((RINGS,)),
            dma((2, 3)), dma((2, 3)), dma((2, 3)), dma((2, 3)), dma((2, 3)), dma((2, 3)),
            dma((RINGS, 2, 4)), dma((RINGS, 2, 4)),
            dma((RINGS, 3, 4)), dma((RINGS, 2, 4)),
            dma, dma, dma, dma, dma, dma,
        ],
        compiler_params=pltpu.CompilerParams(
            collective_id=0, has_side_effects=True, vmem_limit_bytes=62 * 1024 * 1024
        ),
        cost_estimate=pl.CostEstimate(flops=15_000_000_000, bytes_accessed=14_000_000, transcendentals=131072),
        name="expert_backward",
    )(
        row_expert.reshape(1, ROWS), tokens, d_out,
        w_gate_up, w_down.reshape(HID, FEAT),
    )
    grads = (token_grads, gate_up_grads, down_grads.reshape(HID, FEAT))
    token_grads, gate_up_grads, down_grads = pl.pallas_call(
        hand_over,
        out_shape=tuple(jax.ShapeDtypeStruct(g.shape, g.dtype) for g in grads),
        in_specs=[hbm] * 3,
        out_specs=(hbm,) * 3,
        scratch_shapes=[buf(ROWS, FEAT), pltpu.VMEM((1, FEAT, 2, HID), BF16), buf(HID, FEAT), dma((2, 7))],
        name="hand_over",
    )(*grads)
    return token_grads, gate_up_grads, down_grads.reshape(1, HID, FEAT)


def solution(mesh):
    return jax.shard_map(
        local,
        mesh=mesh,
        in_specs=(
            P("exp", "grp"),
            P("exp", "grp"),
            P("exp"),
            P("exp", "grp", None, None),
            P("exp", None, "grp"),
        ),
        out_specs=(P("exp", "grp"), P("exp", "grp", None, None), P("exp", None, "grp")),
        check_vma=False,
    )
```

time: 219 us -> 183 us (0.84)
  the two profiles are of different devices: /device:TPU:24 before, /device:TPU:1 now
where the time goes in v2:
time: 183 us
  Pallas kernels  182 us (99%)
    pallas_call x1, Pallas kernels, local(): pl.pallas_call(kernel, out_shape=(jax.ShapeDtypeStruct((ROWS, FEAT), BF16...  177 us
    pallas_call x1, Pallas kernels, local(): pl.pallas_call(hand_over, out_shape=tuple((jax.ShapeDtypeStruct(g.shape,...  5.24 us

profile of v2, /device:TPU:1, one launch (start us, length us, event | category | flops | bytes accessed | tf_op | source)
XLA Modules:
  0.0 182.8 jit_solution(10571586625867807677)
XLA Ops:
  0.6 176.8 %expert_backward.1 = (bf16[256,896]{1,0:T(8,128)(2,1)}, bf16[1,896,2,1024]{3,2,1,0:T(2,128)(2,1)}, bf16[1024,896]{1,0:T(8,128)(2,1)}) custom-call(s32[1,256]{1,0:T(1,128)} %bitcast.5, bf16[256,896]{1,0:T(8,128)(2,1)} %tok_ref.1, bf16[256,896]{1,0:T(8,128)(2,1)} %dout_ref.1, bf16[1,896,2,1024]{3,2,1,0:T(2,128)(2,1)} %wgu_hbm.1, bf16[1024,896]{1,0:T(8,128)(2,1)} %bitcast.3), custom_call_target="tpu_custom_call" | custom-call | flops 15000000512 | bytes 14000000 | tf_op jit(solution)/shard_map/expert_backward/pallas_call | solution.py:691
  177.4 5.2 %hand_over.1 = (bf16[256,896]{1,0:T(8,128)(2,1)}, bf16[1,896,2,1024]{3,2,1,0:T(2,128)(2,1)}, bf16[1024,896]{1,0:T(8,128)(2,1)}) custom-call(bf16[256,896]{1,0:T(8,128)(2,1)} %get-tuple-element.9.tg, bf16[1,896,2,1024]{3,2,1,0:T(2,128)(2,1)} %get-tuple-element.10.gug, bf16[1024,896]{1,0:T(8,128)(2,1)} %get-tuple-element.11.dg), custom_call_target="tpu_custom_call" | custom-call | tf_op jit(solution)/shard_map/hand_over/pallas_call | solution.py:735

commit v3 on v2

--- a/solution.py
+++ b/solution.py
@@ -157,17 +157,14 @@
                 def _():
                     base_block(k, p)
 
-            if k < 2:
-
-                @pl.when(n > 0)
-                def _():
-                    further_block(k * CAP, 2 * n)
-
-                further_block(k * CAP, 2 * n + 1)
 
     def left(k):
         for n, buf in enumerate((sendx, sendd)):
             many(buf, (8 if k else 7) * CAP, base_send.at[n, k], base_recv.at[n, k]).wait_send()
+
+    @pl.loop(1, HALF)
+    def _(p):
+        further_block(0, p)
 
     stage_d(0)
     xin[0:CAP, :] = sendx[rows(me_e * CAP, CAP), :]
@@ -183,6 +180,11 @@
     w2.wait()
     for copy in ovz:
         copy.wait_recv()
+
+    @pl.loop(1, HALF)
+    def _(p):
+        further_block(CAP, p)
+
     stage_d(1)
     xin[rows(over_place, 2 * CAP), :] = ovx[...]
     din[rows(over_place, 2 * CAP), :] = ovd[...]
@@ -497,21 +499,21 @@
     stage_d(2)
     base_rows(0)
     stage_p(0)
+    stage_c(0)
+    stage_e(0)
     left(1)
     stage_d(3)
     base_rows(1)
     stage_p(1)
+    stage_c(1)
+    stage_e(1)
     hot_rows()
     stage_po(0)
+    stage_m1(0)
     stage_po(1)
-    stage_c(0)
-    stage_e(0)
-    stage_c(1)
-    stage_e(1)
+    stage_m1(1)
     stage_co(0)
     stage_co(1)
-    stage_m1(0)
-    stage_m1(1)
     stage_m2(0)
     stage_m2(1)
     stage_f(0)
@@ -519,6 +521,9 @@
     base_rows(2)
     stage_p(2)
     stage_c(2)
+    base_rows(3)
+    stage_p(3)
+    stage_c(3)
     stage_xo(0)
     stage_xo(1)
     stage_e(4)
@@ -531,19 +536,16 @@
     stage_a(1, 2)
     stage_m2(4)
     stage_m2(5)
+    stage_e(2)
+    stage_e(3)
     stage_a(0, 3)
     stage_a(1, 3)
     stage_f(4)
     stage_f(5)
-    base_rows(3)
-    stage_p(3)
-    stage_c(3)
-    stage_e(2)
-    stage_e(3)
+    stage_m1(2)
+    stage_m1(3)
     stage_a(4, 1)
     stage_a(5, 1)
-    stage_m1(2)
-    stage_m1(3)
     stage_a(4, 2)
     stage_a(5, 2)
     stage_m2(2)
@@ -555,16 +557,16 @@
     stage_f(2)
     stage_f(3)
     stage_g(0)
-    stage_g(1)
     stage_a(2, 1)
     stage_a(3, 1)
-    stage_a(2, 2)
-    stage_a(3, 2)
-    stage_a(2, 3)
-    stage_a(3, 3)
     stage_y(0)
     stage_y(1)
     stage_go()
+    stage_a(2, 2)
+    stage_a(3, 2)
+    stage_g(1)
+    stage_a(2, 3)
+    stage_a(3, 3)
     stage_g(2)
     stage_g(3)
 

time: 183 us -> 164 us (0.90)
  the two profiles are of different devices: /device:TPU:1 before, /device:TPU:24 now
where the time goes in v3:
time: 164 us; the launch traced here: 161 us
  Pallas kernels  160 us (98%)
    pallas_call x1, Pallas kernels, local(): pl.pallas_call(kernel, out_shape=(jax.ShapeDtypeStruct((ROWS, FEAT), BF16...  155 us
    pallas_call x1, Pallas kernels, local(): pl.pallas_call(hand_over, out_shape=tuple((jax.ShapeDtypeStruct(g.shape,...  5.24 us

profile of v3, /device:TPU:24, one launch (start us, length us, event | category | flops | bytes accessed | tf_op | source)
XLA Modules:
  0.0 161.0 jit_solution(14102601444890779521)
XLA Ops:
  0.6 155.0 %expert_backward.1 = (bf16[256,896]{1,0:T(8,128)(2,1)}, bf16[1,896,2,1024]{3,2,1,0:T(2,128)(2,1)}, bf16[1024,896]{1,0:T(8,128)(2,1)}) custom-call(s32[1,256]{1,0:T(1,128)} %bitcast.5, bf16[256,896]{1,0:T(8,128)(2,1)} %tok_ref.1, bf16[256,896]{1,0:T(8,128)(2,1)} %dout_ref.1, bf16[1,896,2,1024]{3,2,1,0:T(2,128)(2,1)} %wgu_hbm.1, bf16[1024,896]{1,0:T(8,128)(2,1)} %bitcast.3), custom_call_target="tpu_custom_call" | custom-call | flops 15000000512 | bytes 14000000 | tf_op jit(solution)/shard_map/expert_backward/pallas_call | solution.py:693
  155.6 5.2 %hand_over.1 = (bf16[256,896]{1,0:T(8,128)(2,1)}, bf16[1,896,2,1024]{3,2,1,0:T(2,128)(2,1)}, bf16[1024,896]{1,0:T(8,128)(2,1)}) custom-call(bf16[256,896]{1,0:T(8,128)(2,1)} %get-tuple-element.9.tg, bf16[1,896,2,1024]{3,2,1,0:T(2,128)(2,1)} %get-tuple-element.10.gug, bf16[1024,896]{1,0:T(8,128)(2,1)} %get-tuple-element.11.dg), custom_call_target="tpu_custom_call" | custom-call | tf_op jit(solution)/shard_map/hand_over/pallas_call | solution.py:737

commit v4 on v3

--- a/solution.py
+++ b/solution.py
@@ -521,9 +521,6 @@
     base_rows(2)
     stage_p(2)
     stage_c(2)
-    base_rows(3)
-    stage_p(3)
-    stage_c(3)
     stage_xo(0)
     stage_xo(1)
     stage_e(4)
@@ -537,15 +534,18 @@
     stage_m2(4)
     stage_m2(5)
     stage_e(2)
-    stage_e(3)
     stage_a(0, 3)
     stage_a(1, 3)
     stage_f(4)
     stage_f(5)
+    base_rows(3)
+    stage_p(3)
+    stage_c(3)
+    stage_e(3)
     stage_m1(2)
-    stage_m1(3)
     stage_a(4, 1)
     stage_a(5, 1)
+    stage_m1(3)
     stage_a(4, 2)
     stage_a(5, 2)
     stage_m2(2)
@@ -564,10 +564,10 @@
     stage_go()
     stage_a(2, 2)
     stage_a(3, 2)
+    stage_a(2, 3)
+    stage_g(2)
     stage_g(1)
-    stage_a(2, 3)
     stage_a(3, 3)
-    stage_g(2)
     stage_g(3)
 
     def gate_up_grads():

time: 164 us -> 158 us (0.963); the launches traced: 161 us -> 157 us
  Pallas kernels: 160 us -> 156 us
    pallas_call x1, Pallas kernels: 155 us -> 151 us  [local(): pl.pallas_call(kernel, out_shape=(jax.ShapeDtypeStruct((ROWS, FEAT), BF16...]
where the time goes in v4:
time: 158 us; the launch traced here: 157 us
  Pallas kernels  156 us (99%)
    pallas_call x1, Pallas kernels, local(): pl.pallas_call(kernel, out_shape=(jax.ShapeDtypeStruct((ROWS, FEAT), BF16...  151 us
    pallas_call x1, Pallas kernels, local(): pl.pallas_call(hand_over, out_shape=tuple((jax.ShapeDtypeStruct(g.shape,...  5.24 us

profile of v4, /device:TPU:24, one launch (start us, length us, event | category | flops | bytes accessed | tf_op | source)
XLA Modules:
  0.0 157.1 jit_solution(10052967342644347857)
XLA Ops:
  0.6 151.1 %expert_backward.1 = (bf16[256,896]{1,0:T(8,128)(2,1)}, bf16[1,896,2,1024]{3,2,1,0:T(2,128)(2,1)}, bf16[1024,896]{1,0:T(8,128)(2,1)}) custom-call(s32[1,256]{1,0:T(1,128)} %bitcast.5, bf16[256,896]{1,0:T(8,128)(2,1)} %tok_ref.1, bf16[256,896]{1,0:T(8,128)(2,1)} %dout_ref.1, bf16[1,896,2,1024]{3,2,1,0:T(2,128)(2,1)} %wgu_hbm.1, bf16[1024,896]{1,0:T(8,128)(2,1)} %bitcast.3), custom_call_target="tpu_custom_call" | custom-call | flops 15000000512 | bytes 14000000 | tf_op jit(solution)/shard_map/expert_backward/pallas_call | solution.py:693
  151.7 5.2 %hand_over.1 = (bf16[256,896]{1,0:T(8,128)(2,1)}, bf16[1,896,2,1024]{3,2,1,0:T(2,128)(2,1)}, bf16[1024,896]{1,0:T(8,128)(2,1)}) custom-call(bf16[256,896]{1,0:T(8,128)(2,1)} %get-tuple-element.9.tg, bf16[1,896,2,1024]{3,2,1,0:T(2,128)(2,1)} %get-tuple-element.10.gug, bf16[1024,896]{1,0:T(8,128)(2,1)} %get-tuple-element.11.dg), custom_call_target="tpu_custom_call" | custom-call | tf_op jit(solution)/shard_map/hand_over/pallas_call | solution.py:737
